TPU v7x, 512 devices: a whole 4x8x8 slice. The times are simulated.
512 devices in a mesh: seq: 64 (over z_hi, y, core), head: 8 (over z_lo, x).
Axes of the slice: x: 4, y: 8, z: 8 (z_hi: 4, z_lo: 2; z = z_hi * 2 + z_lo), core: 2. Of those that a mesh axis runs over, the one named last changes fastest.
Arguments:
- query_feats: bfloat16 [32768, 4096], P('seq', 'head'), may hold values from -16 to 16
- key_feats: bfloat16 [32768, 1024], P('seq', 'head'), may hold values from -7 to 7
- value_feats: bfloat16 [32768, 1024], P('seq', 'head'), may hold values from -6 to 6
- span_class: int32 [32], replicated, may hold values from 1 to 16, as said below
- ramp_width: int32 [32], replicated, may hold values from 32 to 128
- doc_lengths: int32 [16], replicated, may hold values from 1 to 16384, 32768 in all
- out_proj: bfloat16 [4096, 4096], P('seq', 'head'), may hold values from -0.5 to 0.5
Outputs:
- mixed: bfloat16 [32768, 4096], P(('seq', 'head'))
Inputs may be any that keep to these rules, and one draw needn't show every extreme that they name: `span_class`: some head has a span of 16 tiles.
All inputs are finite; a program needn't handle non-finite values.
Results may differ from a plain program's by a relative error of at most 0.014.
Values may be sent and summed in bfloat16 or wider, within the bound.
A program may use at most 64 MiB of HBM per device.

v0:
```python
from functools import partial
import math
import jax
import jax.numpy as jnp
from jax import lax
from jax.sharding import PartitionSpec as P

HD = 128
TILE = 128
BACK = 4
very_low = -1e30


def shifted(block, axis, distance):
    devices = range(lax.axis_size(axis))
    route = [(i - distance, i) for i in devices if i - distance in devices]
    return lax.ppermute(block, axis, route)


def attend(running, key_pair, key_start, context):
    queries, query_pos, doc_start, span_end, ramp_float = context
    top_score, denominator, numerator = running
    tok_rows, kv_count, ratio, head_dim = queries.shape
    key_block = key_pair[0].reshape(tok_rows, kv_count, head_dim)
    value_block = key_pair[1].reshape(tok_rows, kv_count, head_dim)
    scores = jnp.einsum(
        "qgrd,kgd->qgrk", queries, key_block, preferred_element_type=jnp.float32
    ) * (1.0 / math.sqrt(head_dim))
    key_pos = key_start + jnp.arange(tok_rows, dtype=jnp.int32)
    distance = query_pos[:, None] - key_pos[None, :]
    visible = (distance >= 0) & (key_pos[None, :] >= doc_start[:, None])
    weights = jnp.clip(
        (span_end[None, :, :, None] - distance[:, None, None, :].astype(jnp.float32))
        / ramp_float[None, :, :, None],
        0.0,
        1.0,
    )
    weights = jnp.where(visible[:, None, None, :], weights, 0.0)
    limited = jnp.where(weights > 0.0, scores, very_low)
    new_top = jnp.maximum(top_score, jnp.max(limited, axis=3))
    rescale = jnp.exp(top_score - new_top)
    prob_terms = weights * jnp.exp(limited - new_top[:, :, :, None])
    denominator = denominator * rescale + jnp.sum(prob_terms, axis=3)
    numerator = numerator * rescale[:, :, :, None] + jnp.einsum(
        "qgrk,kgd->qgrd",
        prob_terms.astype(jnp.bfloat16),
        value_block,
        preferred_element_type=jnp.float32,
    )
    return (new_top, denominator, numerator)


def unchanged(running):
    return running


def on_device(query_feats, key_feats, value_feats, span_class, ramp_width, doc_lengths, out_proj):
    tok_rows = query_feats.shape[0]
    feat_width = query_feats.shape[1]
    head_count = feat_width // HD
    kv_count = key_feats.shape[1] // HD
    ratio = head_count // kv_count
    seq_index = lax.axis_index("seq")
    head_index = lax.axis_index("head")
    query_pos = seq_index * tok_rows + jnp.arange(tok_rows, dtype=jnp.int32)
    starts = jnp.cumsum(doc_lengths) - doc_lengths
    doc_start = jnp.max(
        jnp.where(starts[None, :] <= query_pos[:, None], starts[None, :], 0), axis=1
    )
    local_span = lax.dynamic_slice_in_dim(span_class, head_index * head_count, head_count)
    local_ramp = lax.dynamic_slice_in_dim(ramp_width, head_index * head_count, head_count)
    span_end = (local_span * TILE).astype(jnp.float32).reshape(kv_count, ratio)
    ramp_float = local_ramp.astype(jnp.float32).reshape(kv_count, ratio)
    context = (
        query_feats.reshape(tok_rows, kv_count, ratio, HD),
        query_pos,
        doc_start,
        span_end,
        ramp_float,
    )
    running = (
        jnp.full((tok_rows, kv_count, ratio), very_low, jnp.float32),
        jnp.zeros((tok_rows, kv_count, ratio), jnp.float32),
        jnp.zeros((tok_rows, kv_count, ratio, HD), jnp.float32),
    )
    own_pair = jnp.stack([key_feats, value_feats])
    running = attend(running, own_pair, seq_index * tok_rows, context)
    reach_most = jnp.max(span_end)
    moving = own_pair
    for offset in range(1, BACK + 1):
        moving = shifted(own_pair, "seq", offset)
        needed = reach_most > float((offset - 1) * tok_rows + 1)
        visit_block = partial(
            attend, key_pair=moving, key_start=(seq_index - offset) * tok_rows, context=context
        )
        running = lax.cond(needed, visit_block, unchanged, running)
    top_score, denominator, numerator = running
    attended = (
        (numerator / denominator[:, :, :, None]).astype(jnp.bfloat16).reshape(tok_rows, feat_width)
    )
    partials = lax.dot_general(
        attended,
        lax.all_gather(out_proj, "seq", axis=0, tiled=True),
        (((1,), (1,)), ((), ())),
        preferred_element_type=jnp.float32,
    )
    mixed_out = lax.psum_scatter(
        partials.astype(jnp.bfloat16), "head", scatter_dimension=0, tiled=True
    )
    return mixed_out


def solution(mesh):
    in_specs = (
        P("seq", "head"),
        P("seq", "head"),
        P("seq", "head"),
        P(),
        P(),
        P(),
        P("seq", "head"),
    )
    out_specs = P(("seq", "head"), None)
    return jax.shard_map(
        on_device, mesh=mesh, in_specs=in_specs, out_specs=out_specs, check_vma=False
    )
```

profile of v0, /device:TPU:1, one launch (start us, length us, event | category | flops | bytes accessed | tf_op | source)
XLA Modules:
  0.0 195.9 jit_solution(2180915210068702400)
XLA Ops:
  6.5 0.7 all-gather.2.cloned.1.call-update
  7.3 1.0 pad_maximum_fusion
  8.3 4.6 %collective-permute-start = (bf16[2,512,128]{2,1,0:T(8,128)(2,1)S(1)}, bf16[2,512,128]{2,1,0:T(8,128)(2,1)S(1)}, u32[]{:S(2)}, u32[]{:S(2)}) collective-permute-start(bf16[2,512,128]{2,1,0:T(8,128)(2,1)S(1)} %pad_maximum_fusion), channel_id=1, source_target_pairs={{0,8},{8,16},{16,24},{24,32},{32,40},{40,48},{48,56},{56,64},{64,7... | collective-permute-start | bytes 786440 | tf_op jit(solution)/shard_map/ppermute | solution.py:17
  12.9 3.2 %collective-permute-start.1 = (bf16[2,512,128]{2,1,0:T(8,128)(2,1)S(1)}, bf16[2,512,128]{2,1,0:T(8,128)(2,1)S(1)}, u32[]{:S(2)}, u32[]{:S(2)}) collective-permute-start(bf16[2,512,128]{2,1,0:T(8,128)(2,1)S(1)} %pad_maximum_fusion), channel_id=1, source_target_pairs={{0,16},{8,24},{16,32},{24,40},{32,48},{40,56},{48,64},{56,72},{64,... | collective-permute-start | bytes 786440 | tf_op jit(solution)/shard_map/ppermute | solution.py:17
  16.1 3.2 %collective-permute-start.2 = (bf16[2,512,128]{2,1,0:T(8,128)(2,1)S(1)}, bf16[2,512,128]{2,1,0:T(8,128)(2,1)S(1)}, u32[]{:S(2)}, u32[]{:S(2)}) collective-permute-start(bf16[2,512,128]{2,1,0:T(8,128)(2,1)S(1)} %pad_maximum_fusion), channel_id=1, source_target_pairs={{0,24},{8,32},{16,40},{24,48},{32,56},{40,64},{48,72},{56,80},{64,... | collective-permute-start | bytes 786440 | tf_op jit(solution)/shard_map/ppermute | solution.py:17
  19.3 4.5 %collective-permute-start.3 = (bf16[2,512,128]{2,1,0:T(8,128)(2,1)S(1)}, bf16[2,512,128]{2,1,0:T(8,128)(2,1)S(1)}, u32[]{:S(2)}, u32[]{:S(2)}) collective-permute-start(bf16[2,512,128]{2,1,0:T(8,128)(2,1)S(1)} %pad_maximum_fusion), channel_id=1, source_target_pairs={{0,32},{8,40},{16,48},{24,56},{32,64},{40,72},{48,80},{56,88},{64,... | collective-permute-start | bytes 786440 | tf_op jit(solution)/shard_map/ppermute | solution.py:17
  23.9 0.7 copy.32
  24.8 0.7 sub.333
  25.4 1.3 fusion.118
  26.8 0.7 dynamic-slice_convert_fusion
  28.1 2.7 %fusion.93 = (f32[512,4]{0,1:T(4,128)S(1)}, f32[512,512,4]{1,0,2:T(8,128)S(1)}) fusion(f32[4]{0:T(128)S(1)} %dynamic-slice_convert_fusion, f32[512,512]{0,1:T(8,128)S(1)} %subtract_convert_fusion.4, f32[4]{0:T(128)S(1)} %get-tuple-element.311, pred[512,512]{0,1:T(8,128)(4,1)S(1)} %fusion.107, bf16[512,128]{1,0:T(8,128)(2,1)} %param.16, ...), kind=kOutput, calls=%fused_computation.117 | convolution fusion | flops 276822016 | bytes 6168608 | tf_op jit(solution)/shard_map/qgrd,kgd->qgrk/dot_general | solution.py:26
  30.8 2.2 %fusion.104 = f32[512,1,4,128]{3,0,2,1:T(8,128)S(1)} fusion(f32[512,4]{0,1:T(4,128)S(1)} %get-tuple-element.324, f32[512,512,4]{1,0,2:T(8,128)S(1)} %get-tuple-element.326, f32[4]{0:T(128)S(1)} %dynamic-slice_convert_fusion, f32[512,512]{0,1:T(8,128)S(1)} %subtract_convert_fusion.4, f32[4]{0:T(128)S(1)} %get-tuple-element.311, ...), kind=kOutput, calls=%fused_computation.126 | convolution fusion | flops 279183360 | bytes 6701088 | tf_op jit(solution)/shard_map/qgrk,kgd->qgrd/dot_general | solution.py:44
  33.1 1.9 fusion.97
  37.8 6.4 %conditional.4 = ((f32[512,1,4]{0,2,1:T(4,128)S(1)}, f32[512,1,4]{0,2,1:T(4,128)S(1)}, f32[512,1,4,128]{3,0,2,1:T(8,128)S(1)})) conditional(s32[]{:T(128)} %convert_element_type.87, (f32[512,1,4]{0,2,1:T(4,128)S(1)}, f32[512,1,4]{0,2,1:T(4,128)S(1)}, f32[512,1,4,128]{3,0,2,1:T(8,128)S(1)}) %tuple.37, (s32[512]{0:T(512)S(1)}, s32[]{:T(128)}, ...), branch_computations={%region_5.6_spmd, %region_6.9_spmd} | conditional | flops 568334848 | bytes 20854852 | solution.py:96
  38.3 1.6 fusion
  39.9 1.9 fusion.4
  41.8 2.4 %fusion.8 = f32[512,1,4,128]{3,0,2,1:T(8,128)S(1)} fusion(f32[512,4]{0,1:T(4,128)S(1)} %bitcast.307, f32[512,512,4]{1,0,2:T(8,128)S(1)} %get-tuple-element.317, f32[4]{0:T(128)S(1)} %get-tuple-element.164, f32[512,512]{0,1:T(8,128)S(1)} %subtract_convert_fusion, f32[4]{0:T(128)S(1)} %get-tuple-element.163, pred[512,512]{0,1:T(8,128)(4,1)S(1)} %fusion.11, ...), kind=kOutput, calls=%fused_computation.11 | convolution fusion | flops 279445504 | bytes 7750656 | tf_op jit(solution)/shard_map/cond/branch_1_fun/qgrk,kgd->qgrd/dot_general | solution.py:44
  44.2 6.6 %conditional.5 = ((f32[512,1,4]{0,2,1:T(4,128)S(1)}, f32[512,1,4]{0,2,1:T(4,128)S(1)}, f32[512,1,4,128]{3,0,2,1:T(8,128)S(1)})) conditional(s32[]{:T(128)} %convert_element_type.86, (f32[512,1,4]{0,2,1:T(4,128)S(1)}, f32[512,1,4]{0,2,1:T(4,128)S(1)}, f32[512,1,4,128]{3,0,2,1:T(8,128)S(1)}) %get-tuple-element.349, (s32[512]{0:T(512)S(1)}, ...), branch_computations={%region_9.10_spmd, %region_10.13_spmd} | conditional | flops 568334848 | bytes 20854852 | solution.py:96
  44.9 1.6 fusion.23
  46.5 1.9 fusion.27
  48.4 2.4 %fusion.31 = f32[512,1,4,128]{3,0,2,1:T(8,128)S(1)} fusion(f32[512,4]{0,1:T(4,128)S(1)} %bitcast.309, f32[512,512,4]{1,0,2:T(8,128)S(1)} %get-tuple-element.319, f32[4]{0:T(128)S(1)} %get-tuple-element.174, f32[512,512]{0,1:T(8,128)S(1)} %subtract_convert_fusion.1, f32[4]{0:T(128)S(1)} %get-tuple-element.173, pred[512,512]{0,1:T(8,128)(4,1)S(1)} %fusion.34, ...), kind=kOutput, calls=%fused_computation.39 | convolution fusion | flops 279445504 | bytes 7750656 | tf_op jit(solution)/shard_map/cond/branch_1_fun/qgrk,kgd->qgrd/dot_general | solution.py:44
  51.6 77.0 %all-gather.2.cloned.1.call-done = bf16[4096,512]{1,0:T(8,128)(2,1)} async-done(((bf16[64,512]{1,0:T(8,128)(2,1)}), bf16[4096,512]{1,0:T(8,128)(2,1)}) %all-gather.2.cloned.1.call-update) | async-done | bytes 4194320 | tf_op jit(solution)/shard_map/all_gather | solution.py:103
  128.6 6.6 %convolution_convert_fusion = bf16[512,4096]{1,0:T(8,128)(2,1)} fusion(bf16[512,512]{0,1:T(8,128)(2,1)S(1)} %bitcast.300, bf16[4096,512]{1,0:T(8,128)(2,1)} %all-gather.2.cloned.1.call-done), kind=kOutput, calls=%fused_computation.113 | convolution fusion | flops 2149580800 | bytes 8912896 | tf_op jit(solution)/shard_map/dot_general | solution.py:101
  135.2 53.9 %reduce-scatter.2.cloned.1.call-done = bf16[64,4096]{1,0:T(8,128)(2,1)} async-done(((bf16[512,4096]{1,0:T(8,128)(2,1)}), bf16[64,4096]{1,0:T(8,128)(2,1)}) %reduce-scatter.2.cloned.1.call-update) | async-done | bytes 524304 | tf_op jit(solution)/shard_map/reduce_scatter | solution.py:107
  (36 shorter events, 3.0 us)
Async XLA Ops:
  6.5 122.1 %all-gather.2.cloned.1.call-start = ((), (), s32[]{:S(2)}) async-start(), calls=%async_computation.1 | async-start | bytes 4259840 | tf_op jit(solution)/shard_map/all_gather | solution.py:103
  7.3 181.8 %reduce-scatter.2.cloned.1.call-start = ((), (), s32[]{:S(2)}) async-start(), calls=%async_computation.2 | async-start | bytes 4718592 | tf_op jit(solution)/shard_map/reduce_scatter | solution.py:107
  8.3 29.5 %collective-permute-start = (bf16[2,512,128]{2,1,0:T(8,128)(2,1)S(1)}, bf16[2,512,128]{2,1,0:T(8,128)(2,1)S(1)}, u32[]{:S(2)}, u32[]{:S(2)}) collective-permute-start(bf16[2,512,128]{2,1,0:T(8,128)(2,1)S(1)} %pad_maximum_fusion), channel_id=1, source_target_pairs={{0,8},{8,16},{16,24},{24,32},{32,40},{40,48},{48,56},{56,64},{64,7... | collective-permute-start | bytes 786440 | tf_op jit(solution)/shard_map/ppermute | solution.py:17
  12.9 31.3 %collective-permute-start.1 = (bf16[2,512,128]{2,1,0:T(8,128)(2,1)S(1)}, bf16[2,512,128]{2,1,0:T(8,128)(2,1)S(1)}, u32[]{:S(2)}, u32[]{:S(2)}) collective-permute-start(bf16[2,512,128]{2,1,0:T(8,128)(2,1)S(1)} %pad_maximum_fusion), channel_id=1, source_target_pairs={{0,16},{8,24},{16,32},{24,40},{32,48},{40,56},{48,64},{56,72},{64,... | collective-permute-start | bytes 786440 | tf_op jit(solution)/shard_map/ppermute | solution.py:17
  16.1 34.7 %collective-permute-start.2 = (bf16[2,512,128]{2,1,0:T(8,128)(2,1)S(1)}, bf16[2,512,128]{2,1,0:T(8,128)(2,1)S(1)}, u32[]{:S(2)}, u32[]{:S(2)}) collective-permute-start(bf16[2,512,128]{2,1,0:T(8,128)(2,1)S(1)} %pad_maximum_fusion), channel_id=1, source_target_pairs={{0,24},{8,32},{16,40},{24,48},{32,56},{40,64},{48,72},{56,80},{64,... | collective-permute-start | bytes 786440 | tf_op jit(solution)/shard_map/ppermute | solution.py:17
  19.3 31.5 %collective-permute-start.3 = (bf16[2,512,128]{2,1,0:T(8,128)(2,1)S(1)}, bf16[2,512,128]{2,1,0:T(8,128)(2,1)S(1)}, u32[]{:S(2)}, u32[]{:S(2)}) collective-permute-start(bf16[2,512,128]{2,1,0:T(8,128)(2,1)S(1)} %pad_maximum_fusion), channel_id=1, source_target_pairs={{0,32},{8,40},{16,48},{24,56},{32,64},{40,72},{48,80},{56,88},{64,... | collective-permute-start | bytes 786440 | tf_op jit(solution)/shard_map/ppermute | solution.py:17
  28.1 2.8 %copy-start.1 = (bf16[512,128]{1,0:T(8,128)(2,1)S(1)}, bf16[512,128]{1,0:T(8,128)(2,1)}, u32[]{:S(2)}) copy-start(bf16[512,128]{1,0:T(8,128)(2,1)} %param.17) | copy-start | bytes 393220
  33.1 1.9 copy-start
Sparse Core Ops, SparseCore 0:
  10.7 117.8 all-gather.1
  135.3 53.6 reduce-scatter.1
where the time goes:
time: 196 us
  waiting for transfers between devices  132 us (67%)
  matrix products  19.5 us (10%)
  between operations  16.2 us (8%)
  starting transfers between devices  15.6 us (8%)
  other arithmetic  11.2 us (6%)
    all_gather x1, waiting for transfers between devices, on_device(): lax.all_gather(out_proj, 'seq', axis=0, tiled=True)  77 us
    reduce_scatter x1, waiting for transfers between devices, on_device(): lax.psum_scatter(partials.astype(jnp.bfloat16), 'head', scatter_dimension...  53.9 us
    ppermute x4, starting transfers between devices, shifted(): return lax.ppermute(block, axis, route)  15.6 us
    dot_general x3, matrix products, attend(): jnp.einsum('qgrk,kgd->qgrd', prob_terms.astype(jnp.bfloat16), value_block...  6.95 us
    dot_general x1, matrix products, on_device(): lax.dot_general(attended, lax.all_gather(out_proj, 'seq', axis=0, tiled=T...  6.56 us
    dot_general x3, matrix products, attend(): jnp.einsum('qgrd,kgd->qgrk', queries, key_block, preferred_element_type=j...  5.96 us
    reduce_sum x3, other arithmetic, attend(): denominator = denominator * rescale + jnp.sum(prob_terms, axis=3)  5.65 us
  transfers between devices with their start and end apart: 6, of which 2 were waited for; matrix products, arithmetic and copies ran while one was open for 13% of the time, Pallas kernels for 0%

commit v1 on v0

--- a/solution.py
+++ b/solution.py
@@ -98,9 +98,16 @@
     attended = (
         (numerator / denominator[:, :, :, None]).astype(jnp.bfloat16).reshape(tok_rows, feat_width)
     )
+
+    def case_prepare(body, d_out):
+        plain = jnp.stack([body for _ in range(jax.lax.axis_size("seq"))])
+        out_arr = jax.lax.all_to_all(plain, "seq", split_axis=0, concat_axis=0)
+        g_now = jnp.concatenate(out_arr, axis=d_out)
+        return g_now
+
     partials = lax.dot_general(
         attended,
-        lax.all_gather(out_proj, "seq", axis=0, tiled=True),
+        case_prepare(out_proj, 0),
         (((1,), (1,)), ((), ())),
         preferred_element_type=jnp.float32,
     )

time: 196 us -> 264 us (1.35)
  waiting for transfers between devices: 132 us -> 180 us
  starting transfers between devices: 15.6 us -> 32.2 us
  other arithmetic: 11.2 us -> 8.23 us
  local copies, waits for them, and re-layouts: 1.3 us -> 3.97 us
    ppermute x4, waiting for transfers between devices: 0.01 us -> 87.1 us  [shifted(): return lax.ppermute(block, axis, route)]
    all_gather x1 -> x0, waiting for transfers between devices: 77 us -> none  [on_device(): lax.all_gather(out_proj, 'seq', axis=0, tiled=True)]
    reduce_scatter x1, waiting for transfers between devices: 53.9 us -> 93.2 us  [on_device(): lax.psum_scatter(partials.astype(jnp.bfloat16), 'head', scatter_dimension...]
    all_to_all x0 -> x1, starting transfers between devices: none -> 18 us  [case_prepare(): out_arr = jax.lax.all_to_all(plain, 'seq', split_axis=0, concat_axis=0)]
    another operation x1 -> x2, local copies, waits for them, and re-layouts: 0.73 us -> 3.4 us  [the longest x1 3.31 us: case_prepare(): plain = jnp.stack([body for _ in range(jax.lax.axis_size('seq'))])]
  transfers between devices with their start and end apart: 6 -> 6, of which waited for: 2 -> 2; matrix products, arithmetic and copies ran while one was open for 13% -> 9% of each run, Pallas kernels for 0% -> 0%
where the time goes in v1:
time: 264 us
  waiting for transfers between devices  180 us (68%)
  starting transfers between devices  32.2 us (12%)
  matrix products  22 us (8%)
  between operations  16.2 us (6%)
  other arithmetic  8.23 us (3%)
  local copies, waits for them, and re-layouts  3.97 us (2%)
    reduce_scatter x1, waiting for transfers between devices, on_device(): lax.psum_scatter(partials.astype(jnp.bfloat16), 'head', scatter_dimension...  93.2 us
    ppermute x4, waiting for transfers between devices, shifted(): return lax.ppermute(block, axis, route)  87.1 us
    all_to_all x1, starting transfers between devices, case_prepare(): out_arr = jax.lax.all_to_all(plain, 'seq', split_axis=0, concat_axis=0)  18 us
    ppermute x4, starting transfers between devices, shifted(): return lax.ppermute(block, axis, route)  14.2 us
    dot_general x3, matrix products, attend(): jnp.einsum('qgrk,kgd->qgrd', prob_terms.astype(jnp.bfloat16), value_block...  8.77 us
    dot_general x3, matrix products, attend(): jnp.einsum('qgrd,kgd->qgrk', queries, key_block, preferred_element_type=j...  6.63 us
    dot_general x1, matrix products, on_device(): lax.dot_general(attended, case_prepare(out_proj, 0), (((1,), (1,)), ((),...  6.56 us
    reduce_sum x3, other arithmetic, attend(): denominator = denominator * rescale + jnp.sum(prob_terms, axis=3)  5.65 us
  transfers between devices with their start and end apart: 6, of which 2 were waited for; matrix products, arithmetic and copies ran while one was open for 9% of the time, Pallas kernels for 0%

profile of v1, /device:TPU:1, one launch (start us, length us, event | category | flops | bytes accessed | tf_op | source)
XLA Modules:
  0.0 263.5 jit_solution(3817531715873493998)
XLA Ops:
  6.5 3.3 %stack.11 = bf16[64,64,512]{2,1,0:T(8,128)(2,1)} broadcast(bf16[64,512]{1,0:T(8,128)(2,1)} %param.21), dimensions={1,2} | broadcast | bytes 4259840 | tf_op jit(solution)/shard_map/stack | solution.py:103
  9.9 18.0 %all-to-all-start = ((bf16[64,64,512]{2,1,0:T(8,128)(2,1)}), bf16[64,64,512]{2,1,0:T(8,128)(2,1)}, u32[]{:S(2)}, u32[]{:S(2)}) async-start(bf16[64,64,512]{2,1,0:T(8,128)(2,1)} %stack.11), calls=%async_computation | async-start | bytes 8388608 | tf_op jit(solution)/shard_map/all_to_all | solution.py:104
  28.0 3.5 %collective-permute-start = (bf16[2,512,128]{2,1,0:T(8,128)(2,1)S(1)}, bf16[2,512,128]{2,1,0:T(8,128)(2,1)}, u32[]{:S(2)}, u32[]{:S(2)}) collective-permute-start(bf16[2,512,128]{2,1,0:T(8,128)(2,1)S(1)} %pad_maximum_fusion), channel_id=1, source_target_pairs={{0,8},{8,16},{16,24},{24,32},{32,40},{40,48},{48,56},{56,64},{64,7... | collective-permute-start | bytes 786440 | tf_op jit(solution)/shard_map/ppermute | solution.py:17
  31.5 3.8 %collective-permute-start.1 = (bf16[2,512,128]{2,1,0:T(8,128)(2,1)S(1)}, bf16[2,512,128]{2,1,0:T(8,128)(2,1)}, u32[]{:S(2)}, u32[]{:S(2)}) collective-permute-start(bf16[2,512,128]{2,1,0:T(8,128)(2,1)S(1)} %pad_maximum_fusion), channel_id=1, source_target_pairs={{0,16},{8,24},{16,32},{24,40},{32,48},{40,56},{48,64},{56,72},{64,... | collective-permute-start | bytes 786440 | tf_op jit(solution)/shard_map/ppermute | solution.py:17
  35.3 2.5 collective-permute-start.2
  37.9 4.3 %collective-permute-start.3 = (bf16[2,512,128]{2,1,0:T(8,128)(2,1)S(1)}, bf16[2,512,128]{2,1,0:T(8,128)(2,1)S(1)}, u32[]{:S(2)}, u32[]{:S(2)}) collective-permute-start(bf16[2,512,128]{2,1,0:T(8,128)(2,1)S(1)} %pad_maximum_fusion), channel_id=1, source_target_pairs={{0,32},{8,40},{16,48},{24,56},{32,64},{40,72},{48,80},{56,88},{64,... | collective-permute-start | bytes 786440 | tf_op jit(solution)/shard_map/ppermute | solution.py:17
  42.4 0.7 fusion.118
  43.3 0.3 fusion.107
  43.8 1.6 fusion.93
  45.4 2.2 fusion.104
  47.6 1.9 fusion.97
  52.3 87.1 %collective-permute-done = bf16[2,512,128]{2,1,0:T(8,128)(2,1)} collective-permute-done((bf16[2,512,128]{2,1,0:T(8,128)(2,1)S(1)}, bf16[2,512,128]{2,1,0:T(8,128)(2,1)}, u32[]{:S(2)}, u32[]{:S(2)}) %collective-permute-start) | collective-permute-done | bytes 262176 | tf_op jit(solution)/shard_map/ppermute | solution.py:17
  139.4 8.2 %conditional.4 = ((f32[512,1,4]{0,2,1:T(4,128)S(1)}, f32[512,1,4]{0,2,1:T(4,128)S(1)}, f32[512,1,4,128]{3,0,2,1:T(8,128)S(1)})) conditional(s32[]{:T(128)} %convert_element_type.87, (f32[512,1,4]{0,2,1:T(4,128)S(1)}, f32[512,1,4]{0,2,1:T(4,128)S(1)}, f32[512,1,4,128]{3,0,2,1:T(8,128)S(1)}) %tuple.37, (s32[512]{0:T(512)S(1)}, s32[]{:T(128)}, ...), branch_computations={%region_5.6_spmd, %region_6.9_spmd} | conditional | flops 568334848 | bytes 20852868 | solution.py:96
  139.9 2.5 fusion
  142.4 1.9 fusion.4
  144.4 3.3 %fusion.8 = f32[512,1,4,128]{3,0,2,1:T(8,128)S(1)} fusion(f32[512,4]{0,1:T(4,128)S(1)} %bitcast.308, f32[512,512,4]{1,0,2:T(8,128)S(1)} %get-tuple-element.317, f32[4]{0:T(128)S(1)} %get-tuple-element.164, f32[512,512]{0,1:T(8,128)S(1)} %subtract_convert_fusion, f32[4]{0:T(128)S(1)} %get-tuple-element.163, pred[512,512]{0,1:T(8,128)(4,1)S(1)} %fusion.11, ...), kind=kOutput, calls=%fused_computation.11 | convolution fusion | flops 279445504 | bytes 7749664 | tf_op jit(solution)/shard_map/cond/branch_1_fun/qgrk,kgd->qgrd/dot_general | solution.py:44
  147.7 8.2 %conditional.5 = ((f32[512,1,4]{0,2,1:T(4,128)S(1)}, f32[512,1,4]{0,2,1:T(4,128)S(1)}, f32[512,1,4,128]{3,0,2,1:T(8,128)S(1)})) conditional(s32[]{:T(128)} %convert_element_type.86, (f32[512,1,4]{0,2,1:T(4,128)S(1)}, f32[512,1,4]{0,2,1:T(4,128)S(1)}, f32[512,1,4,128]{3,0,2,1:T(8,128)S(1)}) %get-tuple-element.349, (s32[512]{0:T(512)S(1)}, ...), branch_computations={%region_9.10_spmd, %region_10.13_spmd} | conditional | flops 568334848 | bytes 20852868 | solution.py:96
  148.2 2.5 fusion.23
  150.7 1.9 fusion.27
  152.6 3.3 %fusion.31 = f32[512,1,4,128]{3,0,2,1:T(8,128)S(1)} fusion(f32[512,4]{0,1:T(4,128)S(1)} %bitcast.310, f32[512,512,4]{1,0,2:T(8,128)S(1)} %get-tuple-element.319, f32[4]{0:T(128)S(1)} %get-tuple-element.174, f32[512,512]{0,1:T(8,128)S(1)} %subtract_convert_fusion.1, f32[4]{0:T(128)S(1)} %get-tuple-element.173, pred[512,512]{0,1:T(8,128)(4,1)S(1)} %fusion.34, ...), kind=kOutput, calls=%fused_computation.39 | convolution fusion | flops 279445504 | bytes 7749664 | tf_op jit(solution)/shard_map/cond/branch_1_fun/qgrk,kgd->qgrd/dot_general | solution.py:44
  156.2 0.6 conditional.7
  156.2 0.3 copy.46
  156.9 6.6 %convolution_convert_fusion = bf16[512,4096]{1,0:T(8,128)(2,1)} fusion(bf16[512,512]{0,1:T(8,128)(2,1)S(1)} %bitcast.301, bf16[4096,512]{1,0:T(8,128)(2,1)} %bitcast.76), kind=kOutput, calls=%fused_computation.113 | convolution fusion | flops 2149580800 | bytes 8912896 | tf_op jit(solution)/shard_map/dot_general | solution.py:108
  163.5 93.2 %reduce-scatter.2.cloned.1.call-done = bf16[64,4096]{1,0:T(8,128)(2,1)} async-done(((bf16[512,4096]{1,0:T(8,128)(2,1)}), bf16[64,4096]{1,0:T(8,128)(2,1)}) %reduce-scatter.2.cloned.1.call-update) | async-done | bytes 524304 | tf_op jit(solution)/shard_map/reduce_scatter | solution.py:114
  (44 shorter events, 2.2 us)
Async XLA Ops:
  9.8 18.1 %copy-start.1 = (bf16[512,128]{1,0:T(8,128)(2,1)S(1)}, bf16[512,128]{1,0:T(8,128)(2,1)}, u32[]{:S(2)}) copy-start(bf16[512,128]{1,0:T(8,128)(2,1)} %param.16) | copy-start | bytes 393220
  9.9 18.1 %copy-start.2 = (bf16[512,128]{1,0:T(8,128)(2,1)S(1)}, bf16[512,128]{1,0:T(8,128)(2,1)}, u32[]{:S(2)}) copy-start(bf16[512,128]{1,0:T(8,128)(2,1)} %param.17) | copy-start | bytes 393220
  9.9 32.3 %copy-start.3 = (s32[16]{0:T(128)S(1)}, s32[16]{0:T(128)}, u32[]{:S(2)}) copy-start(s32[16]{0:T(128)} %param.20) | copy-start | bytes 196
  9.9 32.6 %copy-start.4 = (s32[32]{0:T(128)S(1)}, s32[32]{0:T(128)}, u32[]{:S(2)}) copy-start(s32[32]{0:T(128)} %param.18) | copy-start | bytes 388
  9.9 33.3 %copy-start.5 = (s32[32]{0:T(128)S(1)}, s32[32]{0:T(128)}, u32[]{:S(2)}) copy-start(s32[32]{0:T(128)} %param.19) | copy-start | bytes 388
  9.9 33.9 %copy-start = (bf16[512,512]{1,0:T(8,128)(2,1)S(1)}, bf16[512,512]{1,0:T(8,128)(2,1)}, u32[]{:S(2)}) copy-start(bf16[512,512]{1,0:T(8,128)(2,1)} %param.15) | copy-start | bytes 1572868
  9.9 147.0 %all-to-all-start = ((bf16[64,64,512]{2,1,0:T(8,128)(2,1)}), bf16[64,64,512]{2,1,0:T(8,128)(2,1)}, u32[]{:S(2)}, u32[]{:S(2)}) async-start(bf16[64,64,512]{2,1,0:T(8,128)(2,1)} %stack.11), calls=%async_computation | async-start | bytes 8388608 | tf_op jit(solution)/shard_map/all_to_all | solution.py:104
  27.9 228.8 %reduce-scatter.2.cloned.1.call-start = ((), (), s32[]{:S(2)}) async-start(), calls=%async_computation.2 | async-start | bytes 4718592 | tf_op jit(solution)/shard_map/reduce_scatter | solution.py:114
  28.0 111.5 %collective-permute-start = (bf16[2,512,128]{2,1,0:T(8,128)(2,1)S(1)}, bf16[2,512,128]{2,1,0:T(8,128)(2,1)}, u32[]{:S(2)}, u32[]{:S(2)}) collective-permute-start(bf16[2,512,128]{2,1,0:T(8,128)(2,1)S(1)} %pad_maximum_fusion), channel_id=1, source_target_pairs={{0,8},{8,16},{16,24},{24,32},{32,40},{40,48},{48,56},{56,64},{64,7... | collective-permute-start | bytes 786440 | tf_op jit(solution)/shard_map/ppermute | solution.py:17
  31.5 116.2 %collective-permute-start.1 = (bf16[2,512,128]{2,1,0:T(8,128)(2,1)S(1)}, bf16[2,512,128]{2,1,0:T(8,128)(2,1)}, u32[]{:S(2)}, u32[]{:S(2)}) collective-permute-start(bf16[2,512,128]{2,1,0:T(8,128)(2,1)S(1)} %pad_maximum_fusion), channel_id=1, source_target_pairs={{0,16},{8,24},{16,32},{24,40},{32,48},{40,56},{48,64},{56,72},{64,... | collective-permute-start | bytes 786440 | tf_op jit(solution)/shard_map/ppermute | solution.py:17
  35.3 120.6 %collective-permute-start.2 = (bf16[2,512,128]{2,1,0:T(8,128)(2,1)S(1)}, bf16[2,512,128]{2,1,0:T(8,128)(2,1)S(1)}, u32[]{:S(2)}, u32[]{:S(2)}) collective-permute-start(bf16[2,512,128]{2,1,0:T(8,128)(2,1)S(1)} %pad_maximum_fusion), channel_id=1, source_target_pairs={{0,24},{8,32},{16,40},{24,48},{32,56},{40,64},{48,72},{56,80},{64,... | collective-permute-start | bytes 786440 | tf_op jit(solution)/shard_map/ppermute | solution.py:17
  37.9 118.3 %collective-permute-start.3 = (bf16[2,512,128]{2,1,0:T(8,128)(2,1)S(1)}, bf16[2,512,128]{2,1,0:T(8,128)(2,1)S(1)}, u32[]{:S(2)}, u32[]{:S(2)}) collective-permute-start(bf16[2,512,128]{2,1,0:T(8,128)(2,1)S(1)} %pad_maximum_fusion), channel_id=1, source_target_pairs={{0,32},{8,40},{16,48},{24,56},{32,64},{40,72},{48,80},{56,88},{64,... | collective-permute-start | bytes 786440 | tf_op jit(solution)/shard_map/ppermute | solution.py:17
Sparse Core Ops, SparseCore 0:
  163.6 93.0 reduce-scatter.1
